TPU v7x, 32 devices: a whole 2x2x4 slice. The times are simulated.
32 devices in a mesh: req: 8 (over z, x), mlp: 4 (over y, core).
Axes of the slice: x: 2, y: 2, z: 4, core: 2. Of those that a mesh axis runs over, the one named last changes fastest.
Arguments:
- patches: bfloat16 [2048, 4, 1664], P('req', 'mlp'), may hold values from -6 to 6
- vis_gain: float32 [1664], replicated, may hold values from 0.1 to 1.9
- vis_proj: bfloat16 [6656, 1664], P('mlp'), may hold values from -0.078125 to 0.078125
- targets: int32 [2048], P('req'), may hold values from 0 to 8191, as said below
- lengths: int32 [8], P('req'), may hold values from 512 to 1024, as said below
- text: bfloat16 [8192, 1664], P('req'), may hold values from -6 to 6
- attn_gain: float32 [1664], replicated, may hold values from 0.1 to 1.9
- wqkv: bfloat16 [1664, 4992], P(None, 'mlp'), as said below
- wo: bfloat16 [1664, 1664], P('mlp'), may hold values from -0.15625 to 0.15625
- mlp_gain: float32 [1664], replicated, may hold values from 0.1 to 1.9
- w_in: bfloat16 [1664, 8192], P('req', 'mlp'), may hold values from -0.15625 to 0.15625
- w_out: bfloat16 [8192, 1664], P('mlp', 'req'), may hold values from -0.0625 to 0.0625
Outputs:
- layer_out: bfloat16 [8192, 1664], P(('req', 'mlp'))
Inputs may be any that keep to these rules, and one draw needn't show every extreme that they name: targets[m] = 1024 * prompt + slot, all distinct, every slot below its prompt's length. The rows of one vision device go to one prompt 64 times at most, and this is reached in every draw. `lengths`: some prompt has length 1024. `wqkv`: projection weights, each within -1.8 to 1.8; a head's query and key columns may be much larger than its value columns.
All inputs are finite; a program needn't handle non-finite values.
Results may differ from a plain program's by a relative error of at most 0.027.
The roundings to bfloat16 on the way count: a program that leaves them out, or rounds other values in their place, can miss the bound.
Values may be sent and summed in bfloat16 or wider, within the bound.
A program may use at most 128 MiB of HBM per device.

v0:
```python
import jax
import jax.numpy as jnp
from jax import lax
from jax.sharding import PartitionSpec as P

HD = 104


def rms_scale(values, gain):
    wide = values.astype(jnp.float32)
    power = jnp.mean(wide * wide, axis=-1, keepdims=True)
    return wide * lax.rsqrt(power + 1e-06) * gain


def shards(
    patches, vis_gain, vis_proj, targets, lengths, text, attn_gain, wqkv, wo, mlp_gain, w_in, w_out
):
    requests = lax.axis_size("req")
    seq_len = text.shape[0]
    width = text.shape[1]
    merged_count = patches.shape[0]
    capacity = 2 * merged_count // requests
    patch_norm = rms_scale(patches[:, 0, :], vis_gain).astype(jnp.bfloat16)
    partial_value = jnp.dot(patch_norm, vis_proj, preferred_element_type=jnp.float32)
    target_req = targets // seq_len
    position = targets % seq_len
    one_hot = (target_req[:, None] == jnp.arange(requests)[None, :]).astype(jnp.int32)
    before = jnp.cumsum(one_hot, axis=0) - one_hot
    rank_in = jnp.sum(before * one_hot, axis=1)
    slot_ids = target_req * capacity + rank_in
    slot_fill = jnp.full((requests * capacity,), -1, jnp.int32).at[slot_ids].set(position)
    slot_fill = slot_fill.reshape(requests, capacity)
    image_rows = lax.psum(partial_value, "mlp").astype(jnp.bfloat16)
    buffer = jnp.zeros((requests * capacity, width), jnp.bfloat16).at[slot_ids].set(image_rows)
    buffer = buffer.reshape(requests, capacity, width)
    received, got_slots = (
        lax.all_to_all(buffer, "req", split_axis=0, concat_axis=0, tiled=True),
        lax.all_to_all(slot_fill, "req", split_axis=0, concat_axis=0, tiled=True),
    )
    arrived = received.reshape(requests * capacity, width)
    flat_slots = got_slots.reshape(-1)
    flat_slots = jnp.where(flat_slots < 0, seq_len, flat_slots)
    embedded = text.at[flat_slots].set(arrived, mode="drop")
    attn_in = rms_scale(embedded, attn_gain).astype(jnp.bfloat16)
    qkv = jnp.dot(attn_in, wqkv, preferred_element_type=jnp.float32).astype(jnp.bfloat16)
    local_heads = wqkv.shape[1] // (3 * HD)
    qkv = qkv.reshape(seq_len, local_heads, 3, HD)
    query, keys, values = (qkv[:, :, 0], qkv[:, :, 1], qkv[:, :, 2])
    scores = (
        jnp.einsum("qhd,khd->hqk", query, keys, preferred_element_type=jnp.float32)
        / jnp.float32(HD) ** 0.5
    )
    row_ids = jnp.arange(seq_len)
    causal = row_ids[None, :] <= row_ids[:, None]
    scores = jnp.where(causal[None], scores, jnp.float32(-1e30))
    peak = jnp.max(scores, axis=-1, keepdims=True)
    weights = jnp.exp(scores - peak)
    probs = (weights / jnp.sum(weights, axis=-1, keepdims=True)).astype(jnp.bfloat16)
    context = jnp.einsum("hqk,khd->qhd", probs, values, preferred_element_type=jnp.float32).astype(
        jnp.bfloat16
    )
    context = context.reshape(seq_len, local_heads * HD)
    attn_part = jnp.dot(context, wo, preferred_element_type=jnp.float32)
    group = lax.axis_index("mlp")
    share_rows = seq_len // lax.axis_size("mlp")
    share_start = group * share_rows
    attn_total = lax.psum(attn_part.astype(jnp.bfloat16), "mlp").astype(jnp.float32)
    resid_all = embedded.astype(jnp.float32) + attn_total
    mlp_in = rms_scale(resid_all, mlp_gain).astype(jnp.bfloat16)
    resid_share = lax.dynamic_slice_in_dim(resid_all, share_start, share_rows, 0)
    upward = jnp.dot(
        mlp_in, lax.all_gather(w_in, "req", axis=0, tiled=True), preferred_element_type=jnp.float32
    )
    active = jax.nn.gelu(upward, approximate=False).astype(jnp.bfloat16)
    mlp_part = jnp.dot(
        active, lax.all_gather(w_out, "req", axis=1, tiled=True), preferred_element_type=jnp.float32
    )
    mlp_share = lax.psum_scatter(
        mlp_part.astype(jnp.bfloat16), "mlp", scatter_dimension=0, tiled=True
    ).astype(jnp.float32)
    result = resid_share + mlp_share
    share_ids = share_start + jnp.arange(share_rows)
    valid = share_ids < lengths[0]
    return jnp.where(valid[:, None], result, jnp.float32(0.0)).astype(jnp.bfloat16)


def solution(mesh):
    return jax.shard_map(
        shards,
        mesh=mesh,
        in_specs=(
            P("req", "mlp", None),
            P(),
            P("mlp", None),
            P("req"),
            P("req"),
            P("req", None),
            P(),
            P(None, "mlp"),
            P("mlp", None),
            P(),
            P("req", "mlp"),
            P("mlp", "req"),
        ),
        out_specs=P(("req", "mlp"), None),
        check_vma=False,
    )
```

profile of v0, /device:TPU:0, one launch (start us, length us, event | category | flops | bytes accessed | tf_op | source)
XLA Modules:
  0.0 462.8 jit_solution(4514152657688184851)
XLA Ops:
  7.4 0.0 copy-start
  7.4 0.0 all-reduce.3.cloned.1.call-start
  7.4 0.0 copy-start.5
  7.4 4.1 copy.30
  11.5 0.0 copy-done.3
  11.5 0.2 fusion.32
  11.8 0.0 copy-done.6
  11.8 0.8 copy-done.5
  12.6 3.1 fusion.36
  15.7 0.0 all-reduce.3.cloned.1.call-update
  15.7 0.6 reduce-window.6
  16.3 0.2 slice_reduce_fusion
  16.6 0.1 fusion.46
  16.7 1.4 scatter_custom_fusion
  18.1 0.7 all_to_all.9
  18.8 7.3 %all-to-all-start = ((s32[8,1,64]{2,1,0:T(1,128)}), s32[8,1,64]{2,1,0:T(1,128)S(1)}, u32[]{:S(2)}, u32[]{:S(2)}) async-start(s32[8,1,64]{2,1,0:T(1,128)} %all_to_all.9), calls=%async_computation | async-start | bytes 8192 | tf_op jit(solution)/shard_map/all_to_all | solution.py:38
  26.0 37.5 %all-reduce.3.cloned.1.call-done = f32[256,1664]{1,0:T(8,128)} async-done(((f32[256,1664]{1,0:T(8,128)}), f32[256,1664]{1,0:T(8,128)}) %all-reduce.3.cloned.1.call-update) | async-done | bytes 1703952 | tf_op jit(solution)/shard_map/psum | solution.py:33
  63.5 4.2 scatter_custom_fusion.1
  67.7 0.0 all-to-all-done
  67.7 5.5 %all-to-all-start.1 = ((bf16[8,64,1664]{2,1,0:T(8,128)(2,1)}), bf16[8,64,1664]{2,1,0:T(8,128)(2,1)S(1)}, u32[]{:S(2)}, u32[]{:S(2)}) async-start(bf16[8,64,1664]{2,1,0:T(8,128)(2,1)} %bitcast.67), calls=%async_computation.1 | async-start | bytes 3407872 | tf_op jit(solution)/shard_map/all_to_all | solution.py:37
  73.2 0.0 all-reduce.5.cloned.1.call-start
  73.2 1.3 iota_compare_fusion
  74.6 0.5 broadcast.168
  75.1 0.7 reduce.5
  75.7 0.1 reshape.113
  75.8 37.0 %all-to-all-done.1 = bf16[8,64,1664]{2,1,0:T(8,128)(2,1)S(1)} async-done(((bf16[8,64,1664]{2,1,0:T(8,128)(2,1)}), bf16[8,64,1664]{2,1,0:T(8,128)(2,1)S(1)}, u32[]{:S(2)}, u32[]{:S(2)}) %all-to-all-start.1) | async-done | bytes 1703968 | tf_op jit(solution)/shard_map/all_to_all | solution.py:37
  112.8 7.6 %scatter_fusion = bf16[1024,1664]{1,0:T(8,128)(2,1)} fusion(bf16[1024,1664]{1,0:T(8,128)(2,1)} %copy.30, s32[512]{0:T(512)S(1)} %bitcast.69, bf16[512,1664]{1,0:T(8,128)(2,1)S(1)} %bitcast.66), kind=kCustom, calls=%fused_computation.2 | custom fusion | bytes 5113856 | tf_op jit(solution)/shard_map/scatter | solution.py:43
  120.4 2.7 fusion.16
  123.2 9.7 %convolution_convert_fusion = bf16[1024,1248]{0,1:T(8,128)(2,1)} fusion(bf16[1664,1248]{0,1:T(8,128)(2,1)} %param.19, bf16[1024,1664]{1,0:T(8,128)(2,1)} %scatter_fusion, f32[1664]{0:T(1024)S(1)} %copy-done.7, f32[1024]{0:T(1024)S(1)} %add_rsqrt_fusion.1), kind=kOutput, calls=%fused_computation.42 | convolution fusion | flops 4261117952 | bytes 10127872 | tf_op jit(solution)/shard_map/dot_general | solution.py:45
  132.8 0.0 copy-done.2
  132.8 11.3 %fusion.82 = (f32[4,1024]{1,0:T(4,128)S(1)}, f32[4,1024,1024]{1,2,0:T(8,128)}) fusion(pred[1024,1024]{0,1:T(8,128)(4,1)S(1)} %copy-done.2, bf16[1024,4,3,104]{0,3,2,1:T(8,128)(2,1)} %bitcast.70), kind=kOutput, calls=%fused_computation.123 | convolution fusion | flops 889193472 | bytes 19546112 | tf_op jit(solution)/shard_map/sub | solution.py:57
  144.2 7.5 %fusion.35 = bf16[4,104,1024]{2,1,0:T(8,128)(2,1)S(1)} fusion(f32[4,1024,1024]{1,2,0:T(8,128)} %get-tuple-element.10, f32[4,1024]{1,0:T(4,128)S(1)} %get-tuple-element.9, bf16[1024,4,3,104]{0,3,2,1:T(8,128)(2,1)} %bitcast.71), kind=kOutput, calls=%fused_computation.56 | convolution fusion | flops 881229824 | bytes 18497536 | tf_op jit(solution)/shard_map/hqk,khd->qhd/dot_general | solution.py:59
  151.6 3.8 convolution_convert_fusion.1
  155.5 0.0 all-reduce.5.cloned.1.call-update
  155.5 0.0 all-gather.3.cloned.1.call-start
  155.6 0.5 all-gather.3.cloned.1.call-update
  156.1 0.0 all-gather.5.cloned.1.call-start
  156.1 0.5 all-gather.5.cloned.1.call-update
  156.7 0.0 copy-start.8
  156.7 0.0 reduce-scatter.2.cloned.1.call-start
  156.7 70.1 %all-reduce.5.cloned.1.call-done = bf16[1024,1664]{1,0:T(8,128)(2,1)} async-done(((bf16[1024,1664]{1,0:T(8,128)(2,1)}), bf16[1024,1664]{1,0:T(8,128)(2,1)}) %all-reduce.5.cloned.1.call-update) | async-done | bytes 3407888 | tf_op jit(solution)/shard_map/psum | solution.py:67
  226.9 6.9 %convert_add_fusion = (f32[1024,1664]{1,0:T(8,128)}, f32[1024]{0:T(1024)S(1)}) fusion(bf16[1024,1664]{1,0:T(8,128)(2,1)} %scatter_fusion, bf16[1024,1664]{1,0:T(8,128)(2,1)} %all-reduce.5.cloned.1.call-done), kind=kLoop, calls=%fused_computation.9 | loop fusion | flops 8518656 | bytes 13635584 | tf_op jit(solution)/shard_map/add | solution.py:68
  233.8 28.0 %all-gather.3.cloned.1.call-done = bf16[1664,2048]{1,0:T(8,128)(2,1)} async-done(((bf16[208,2048]{1,0:T(8,128)(2,1)}), bf16[1664,2048]{1,0:T(8,128)(2,1)}) %all-gather.3.cloned.1.call-update) | async-done | bytes 6815760 | tf_op jit(solution)/shard_map/all_gather | solution.py:72
  261.8 105.4 %all-gather.5.cloned.1.call-done = bf16[2048,1664]{0,1:T(8,128)(2,1)} async-done(((bf16[2048,208]{0,1:T(8,128)(2,1)}), bf16[2048,1664]{0,1:T(8,128)(2,1)}) %all-gather.5.cloned.1.call-update) | async-done | bytes 6815760 | tf_op jit(solution)/shard_map/all_gather | solution.py:76
  367.2 47.5 %fusion.21 = bf16[1024,1664]{1,0:T(8,128)(2,1)} fusion(bf16[2048,1664]{0,1:T(8,128)(2,1)} %all-gather.5.cloned.1.call-done, bf16[1664,2048]{1,0:T(8,128)(2,1)} %all-gather.3.cloned.1.call-done, f32[1664]{0:T(1024)S(1)} %copy-done.8, f32[1024]{0:T(1024)S(1)} %add_rsqrt_fusion, bf16[1024,1664]{1,0:T(8,128)(2,1)} %scatter_fusion, ...), kind=kOutput, calls=%fused_computation.41 | convolution fusion | flops 14106886144 | bytes 23865856 | tf_op jit(solution)/shard_map/dot_general | solution.py:75
  414.7 0.0 reduce-scatter.2.cloned.1.call-update
  415.4 37.3 %reduce-scatter.2.cloned.1.call-done = bf16[256,1664]{1,0:T(8,128)(2,1)} async-done(((bf16[1024,1664]{1,0:T(8,128)(2,1)}), bf16[256,1664]{1,0:T(8,128)(2,1)}) %reduce-scatter.2.cloned.1.call-update) | async-done | bytes 851984 | tf_op jit(solution)/shard_map/reduce_scatter | solution.py:78
  452.6 2.9 select_convert_fusion
  (21 shorter events, 0.1 us)
Async XLA Ops:
  7.4 144.3 %copy-start = (bf16[416,1664]{1,0:T(8,128)(2,1)S(1)}, bf16[416,1664]{1,0:T(8,128)(2,1)}, u32[]{:S(2)}) copy-start(bf16[416,1664]{1,0:T(8,128)(2,1)} %param.20) | copy-start | bytes 4153348
  7.4 4.1 copy-start.3
  7.4 4.4 copy-start.6
  7.4 56.1 %all-reduce.3.cloned.1.call-start = ((), (), s32[]{:S(2)}) async-start(), calls=%async_computation.3 | async-start | bytes 3407872 | tf_op jit(solution)/shard_map/psum | solution.py:33
  7.4 5.2 %copy-start.5 = (bf16[1664,1664]{1,0:T(8,128)(2,1)S(1)}, bf16[1664,1664]{1,0:T(8,128)(2,1)}, u32[]{:S(2)}) copy-start(bf16[1664,1664]{1,0:T(8,128)(2,1)} %param.14) | copy-start | bytes 16613380
  12.6 3.1 copy-start.4
  18.8 48.9 %all-to-all-start = ((s32[8,1,64]{2,1,0:T(1,128)}), s32[8,1,64]{2,1,0:T(1,128)S(1)}, u32[]{:S(2)}, u32[]{:S(2)}) async-start(s32[8,1,64]{2,1,0:T(1,128)} %all_to_all.9), calls=%async_computation | async-start | bytes 8192 | tf_op jit(solution)/shard_map/all_to_all | solution.py:38
  67.7 45.1 %all-to-all-start.1 = ((bf16[8,64,1664]{2,1,0:T(8,128)(2,1)}), bf16[8,64,1664]{2,1,0:T(8,128)(2,1)S(1)}, u32[]{:S(2)}, u32[]{:S(2)}) async-start(bf16[8,64,1664]{2,1,0:T(8,128)(2,1)} %bitcast.67), calls=%async_computation.1 | async-start | bytes 3407872 | tf_op jit(solution)/shard_map/all_to_all | solution.py:37
  73.2 153.7 %all-reduce.5.cloned.1.call-start = ((), (), s32[]{:S(2)}) async-start(), calls=%async_computation.4 | async-start | bytes 6815744 | tf_op jit(solution)/shard_map/psum | solution.py:67
  112.8 10.3 %copy-start.7 = (f32[1664]{0:T(1024)S(1)}, f32[1664]{0:T(1024)}, u32[]{:S(2)}) copy-start(f32[1664]{0:T(1024)} %param.18) | copy-start | bytes 19972
  123.1 9.7 %copy-start.2 = (pred[1024,1024]{0,1:T(8,128)(4,1)S(1)}, pred[1024,1024]{0,1:T(8,128)(4,1)}, u32[]{:S(2)}) copy-start(pred[1024,1024]{0,1:T(8,128)(4,1)} %iota_compare_fusion) | copy-start | bytes 3145732
  155.5 106.3 %all-gather.3.cloned.1.call-start = ((), (), s32[]{:S(2)}) async-start(), calls=%async_computation.5 | async-start | bytes 7667712 | tf_op jit(solution)/shard_map/all_gather | solution.py:72
  156.1 211.1 %all-gather.5.cloned.1.call-start = ((), (), s32[]{:S(2)}) async-start(), calls=%async_computation.6 | async-start | bytes 7667712 | tf_op jit(solution)/shard_map/all_gather | solution.py:76
  156.7 210.5 %copy-start.8 = (f32[1664]{0:T(1024)S(1)}, f32[1664]{0:T(1024)}, u32[]{:S(2)}) copy-start(f32[1664]{0:T(1024)} %param.21) | copy-start | bytes 19972
  156.7 295.9 %reduce-scatter.2.cloned.1.call-start = ((), (), s32[]{:S(2)}) async-start(), calls=%async_computation.7 | async-start | bytes 4259840 | tf_op jit(solution)/shard_map/reduce_scatter | solution.py:78
  367.2 88.3 %copy-start.1 = (bf16[416,1664]{1,0:T(8,128)(2,1)S(1)}, bf16[416,1664]{1,0:T(8,128)(2,1)}, u32[]{:S(2)}) copy-start(bf16[416,1664]{1,0:T(8,128)(2,1)} %param.20) | copy-start | bytes 4153348
Sparse Core Ops, SparseCore 0:
  15.8 47.6 all-reduce.2
  155.6 71.1 all-reduce.4
  414.8 37.7 reduce-scatter.1
Sparse Core Ops, SparseCore 1:
  158.2 103.6 all-gather.2
  263.9 103.3 all-gather.4
where the time goes:
time: 466 us; the launch traced here: 463 us
  waiting for transfers between devices  316 us (68%)
  matrix products  82.9 us (18%)
  other arithmetic  19.6 us (4%)
  between operations  15.5 us (3%)
  local copies, waits for them, and re-layouts  15.4 us (3%)
  starting transfers between devices  12.9 us (3%)
    all_gather x1, waiting for transfers between devices, shards(): lax.all_gather(w_out, 'req', axis=1, tiled=True)  105 us
    psum x1, waiting for transfers between devices, shards(): lax.psum(attn_part.astype(jnp.bfloat16), 'mlp').astype(jnp.float32)  70.1 us
    dot_general x1, matrix products, shards(): jnp.dot(active, lax.all_gather(w_out, 'req', axis=1, tiled=True), preferr...  47.5 us
    psum x1, waiting for transfers between devices, shards(): image_rows = lax.psum(partial_value, 'mlp').astype(jnp.bfloat16)  37.5 us
    reduce_scatter x1, waiting for transfers between devices, shards(): lax.psum_scatter(mlp_part.astype(jnp.bfloat16), 'mlp', scatter_dimension=...  37.3 us
    all_to_all x1, waiting for transfers between devices, shards(): lax.all_to_all(buffer, 'req', split_axis=0, concat_axis=0, tiled=True)  37 us
    all_gather x1, waiting for transfers between devices, shards(): lax.all_gather(w_in, 'req', axis=0, tiled=True)  28 us
    sub x1, matrix products, shards(): weights = jnp.exp(scores - peak)  11.3 us
  transfers between devices with their start and end apart: 7, of which 6 were waited for; matrix products, arithmetic and copies ran while one was open for 3% of the time, Pallas kernels for 0%

commit v1 on v0

v1 whole, which is shorter than its diff:
```python
import jax
import jax.numpy as jnp
from jax import lax
from jax.sharding import PartitionSpec as P

HD = 104
CHUNKS = 2
PHASES = 4


def rms_scale(values, gain):
    wide = values.astype(jnp.float32)
    power = jnp.mean(wide * wide, axis=-1, keepdims=True)
    return wide * lax.rsqrt(power + 1e-06) * gain


def shards(
    patches, vis_gain, vis_proj, targets, lengths, text, attn_gain, wqkv, wo, mlp_gain, w_in, w_out
):
    requests = lax.axis_size("req")
    groups = lax.axis_size("mlp")
    seq_len, width = text.shape
    merged_count = patches.shape[0]
    capacity = 2 * merged_count // requests
    steps = requests // 2
    flip = [(i, i ^ 1) for i in range(requests)]
    onward = [(i, (i + 2) % requests) for i in range(requests)]
    chain = {"hand": (w_in, w_out.T), "pairs": [], "step": 0}

    def advance(phase, tied):
        new = []
        while chain["step"] < (phase + 1) * steps // PHASES:
            hand = chain["hand"]
            across = tuple(lax.ppermute(block, "req", flip) for block in hand)
            chain["pairs"].append([hand, across])
            chain["step"] += 1
            if chain["step"] < steps:
                chain["hand"] = tuple(lax.ppermute(block, "req", onward) for block in hand)
            new.append(len(chain["pairs"]) - 1)
        if tied is None:
            return None
        across = [chain["pairs"][i][1] for i in new]
        tied, across, chain["hand"] = lax.optimization_barrier((tied, across, chain["hand"]))
        for i, value in zip(new, across):
            chain["pairs"][i][1] = value
        return tied

    def gathered(which):
        me = lax.axis_index("req")
        full = jnp.zeros((requests, *chain["pairs"][0][0][which].shape), jnp.bfloat16)
        for step, (own, across) in enumerate(chain["pairs"]):
            source = (me - 2 * step) % requests
            full = lax.dynamic_update_index_in_dim(full, own[which], source, 0)
            full = lax.dynamic_update_index_in_dim(full, across[which], source ^ 1, 0)
        return full.reshape(-1, full.shape[-1])

    patch_norm = rms_scale(patches[:, 0, :], vis_gain).astype(jnp.bfloat16)
    partial_value = jnp.dot(patch_norm, vis_proj, preferred_element_type=jnp.float32)
    image_rows = lax.psum(partial_value.astype(jnp.bfloat16), "mlp")
    image_rows = advance(0, image_rows)
    target_req = targets // seq_len
    position = targets % seq_len
    order = jnp.arange(merged_count)
    same = (target_req[:, None] == target_req[None, :]) & (order[None, :] < order[:, None])
    rank_in = jnp.sum(same.astype(jnp.int32), axis=1)
    slot_ids = target_req * capacity + rank_in
    pick = slot_ids[None, :] == jnp.arange(requests * capacity)[:, None]
    slot_fill = jnp.max(jnp.where(pick, position[None, :], -1), axis=1).reshape(requests, capacity)
    got_slots = lax.all_to_all(slot_fill, "req", split_axis=0, concat_axis=0, tiled=True)
    buffer = jnp.dot(
        pick.astype(jnp.bfloat16), image_rows, preferred_element_type=jnp.float32
    ).astype(jnp.bfloat16)
    received = lax.all_to_all(
        buffer.reshape(requests, capacity, width), "req", split_axis=0, concat_axis=0, tiled=True
    )
    received = advance(1, received)
    arrived = received.reshape(requests * capacity, width)
    place = got_slots.reshape(-1)[None, :] == jnp.arange(seq_len)[:, None]
    placed = jnp.dot(place.astype(jnp.bfloat16), arrived, preferred_element_type=jnp.float32)
    hit = jnp.any(place, axis=1, keepdims=True)
    embedded = jnp.where(hit, placed.astype(jnp.bfloat16), text)

    attn_in = rms_scale(embedded, attn_gain).astype(jnp.bfloat16)
    qkv = jnp.dot(attn_in, wqkv, preferred_element_type=jnp.float32).astype(jnp.bfloat16)
    qkv = advance(2, qkv)
    advance(3, None)
    local_heads = wqkv.shape[1] // (3 * HD)
    qkv = qkv.reshape(seq_len, local_heads, 3, HD)
    query, keys, values = (qkv[:, :, 0], qkv[:, :, 1], qkv[:, :, 2])
    share_rows = seq_len // groups
    piece = share_rows // CHUNKS

    def chunk_of(array, j):
        cut = array.reshape(groups, CHUNKS, piece, *array.shape[1:])[:, j]
        return cut.reshape(groups * piece, *array.shape[1:])

    row_ids = jnp.arange(seq_len)
    sums = []
    for j in range(CHUNKS):
        rows = chunk_of(row_ids, j)
        scores = (
            jnp.einsum("qhd,khd->hqk", chunk_of(query, j), keys, preferred_element_type=jnp.float32)
            / jnp.float32(HD) ** 0.5
        )
        causal = row_ids[None, :] <= rows[:, None]
        scores = jnp.where(causal[None], scores, jnp.float32(-1e30))
        peak = jnp.max(scores, axis=-1, keepdims=True)
        weights = jnp.exp(scores - peak)
        probs = (weights / jnp.sum(weights, axis=-1, keepdims=True)).astype(jnp.bfloat16)
        context = jnp.einsum(
            "hqk,khd->qhd", probs, values, preferred_element_type=jnp.float32
        ).astype(jnp.bfloat16)
        context = context.reshape(groups * piece, local_heads * HD)
        attn_part = jnp.dot(context, wo, preferred_element_type=jnp.float32)
        sums.append(
            lax.psum_scatter(
                attn_part.astype(jnp.bfloat16), "mlp", scatter_dimension=0, tiled=True
            )
        )
    group = lax.axis_index("mlp")
    own_embedded = lax.dynamic_slice_in_dim(embedded, group * share_rows, share_rows, 0)
    resids, inputs = [], []
    for j in range(CHUNKS):
        own = own_embedded[j * piece : (j + 1) * piece]
        resid = own.astype(jnp.float32) + sums[j].astype(jnp.float32)
        resids.append(resid)
        mlp_in = rms_scale(resid, mlp_gain).astype(jnp.bfloat16)
        inputs.append(lax.all_gather(mlp_in, "mlp", axis=0, tiled=True))
    w_in_full, w_out_full = gathered(0), gathered(1)
    outs = []
    for j in range(CHUNKS):
        mlp_in = inputs[j]
        upward = jnp.dot(mlp_in, w_in_full, preferred_element_type=jnp.float32)
        active = jax.nn.gelu(upward, approximate=False).astype(jnp.bfloat16)
        mlp_part = lax.dot_general(
            active, w_out_full, (((1,), (1,)), ((), ())), preferred_element_type=jnp.float32
        )
        mlp_share = lax.psum_scatter(
            mlp_part.astype(jnp.bfloat16), "mlp", scatter_dimension=0, tiled=True
        ).astype(jnp.float32)
        result = resids[j] + mlp_share
        ids = group * share_rows + j * piece + jnp.arange(piece)
        outs.append(jnp.where((ids < lengths[0])[:, None], result, 0.0).astype(jnp.bfloat16))
    return jnp.concatenate(outs, axis=0)


def solution(mesh):
    return jax.shard_map(
        shards,
        mesh=mesh,
        in_specs=(
            P("req", "mlp", None),
            P(),
            P("mlp", None),
            P("req"),
            P("req"),
            P("req", None),
            P(),
            P(None, "mlp"),
            P("mlp", None),
            P(),
            P("req", "mlp"),
            P("mlp", "req"),
        ),
        out_specs=P(("req", "mlp"), None),
        check_vma=False,
    )
```

time: 466 us -> 389 us (0.83)
  waiting for transfers between devices: 316 us -> 196 us
  local copies, waits for them, and re-layouts: 15.4 us -> 37.8 us
  starting transfers between devices: 12.9 us -> 29.2 us
  matrix products: 82.9 us -> 92.6 us
  other arithmetic: 19.6 us -> 11.4 us
    all_gather x2, waiting for transfers between devices: 133 us -> 8.88 us  [shards(): inputs.append(lax.all_gather(mlp_in, 'mlp', axis=0, tiled=True))]
    ppermute x0 -> x14, waiting for transfers between devices: none -> 86.8 us  [the longest x8 50.5 us: advance(): across = tuple((lax.ppermute(block, 'req', flip) for block in hand))]
    psum x2 -> x1, waiting for transfers between devices: 108 us -> 29.5 us  [shards(): image_rows = lax.psum(partial_value.astype(jnp.bfloat16), 'mlp')]
    all_to_all x1, waiting for transfers between devices: 37 us -> 8.12 us  [shards(): lax.all_to_all(buffer.reshape(requests, capacity, width), 'req', split_ax...]
    dynamic_update_slice x0 -> x15, local copies, waits for them, and re-layouts: none -> 24.6 us  [the longest x7 14.9 us: gathered(): full = lax.dynamic_update_index_in_dim(full, across[which], source ^ 1, 0)]
    reduce_scatter x0 -> x2, waiting for transfers between devices: none -> 21.1 us  [shards(): lax.psum_scatter(attn_part.astype(jnp.bfloat16), 'mlp', scatter_dimension...]
    ppermute x0 -> x14, starting transfers between devices: none -> 18.4 us  [the longest x8 10.6 us: advance(): across = tuple((lax.ppermute(block, 'req', flip) for block in hand))]
    scatter x2 -> x0, local copies, waits for them, and re-layouts: 9.01 us -> none  [the longest x1 7.62 us: shards(): embedded = text.at[flat_slots].set(arrived, mode='drop')]
  transfers between devices with their start and end apart: 7 -> 23, of which waited for: 6 -> 13; matrix products, arithmetic and copies ran while one was open for 3% -> 30% of each run, Pallas kernels for 0% -> 0%
where the time goes in v1:
time: 389 us; the launch traced here: 382 us
  waiting for transfers between devices  196 us (50%)
  matrix products  92.6 us (24%)
  local copies, waits for them, and re-layouts  37.8 us (10%)
  starting transfers between devices  29.2 us (8%)
  between operations  15 us (4%)
  other arithmetic  11.4 us (3%)
    ppermute x8, waiting for transfers between devices, advance(): across = tuple((lax.ppermute(block, 'req', flip) for block in hand))  50.5 us
    dot_general x2, matrix products, shards(): lax.dot_general(active, w_out_full, (((1,), (1,)), ((), ())), preferred_e...  42.4 us
    reduce_scatter x2, waiting for transfers between devices, shards(): lax.psum_scatter(mlp_part.astype(jnp.bfloat16), 'mlp', scatter_dimension=...  41.3 us
    ppermute x6, waiting for transfers between devices, advance(): lax.ppermute(block, 'req', onward)  36.3 us
    psum x1, waiting for transfers between devices, shards(): image_rows = lax.psum(partial_value.astype(jnp.bfloat16), 'mlp')  29.5 us
    reduce_scatter x2, waiting for transfers between devices, shards(): lax.psum_scatter(attn_part.astype(jnp.bfloat16), 'mlp', scatter_dimension...  21.1 us
    sub x2, matrix products, shards(): weights = jnp.exp(scores - peak)  15.3 us
    dynamic_update_slice x7, local copies, waits for them, and re-layouts, gathered(): full = lax.dynamic_update_index_in_dim(full, across[which], source ^ 1, 0)  14.9 us
  transfers between devices with their start and end apart: 23, of which 13 were waited for; matrix products, arithmetic and copies ran while one was open for 30% of the time, Pallas kernels for 0%

profile of v1, /device:TPU:0, one launch (start us, length us, event | category | flops | bytes accessed | tf_op | source)
XLA Modules:
  0.0 381.8 jit_solution(6332397471049983945)
XLA Ops:
  6.5 2.9 collective-permute-start.1
  9.5 1.6 collective-permute-start.3
  11.6 1.6 collective-permute-start.2
  14.6 5.6 %convolution_convert_fusion.7 = bf16[256,1664]{1,0:T(8,128)(2,1)} fusion(bf16[1664,1664]{1,0:T(8,128)(2,1)} %param.14, bf16[256,1,1664]{2,0,1:T(8,128)(2,1)} %param.12, f32[1664]{0:T(1024)} %param.13, f32[256]{0:T(256)S(1)} %add_rsqrt_fusion.1), kind=kOutput, calls=%fused_computation.71 | convolution fusion | flops 1419804672 | bytes 7249408 | tf_op jit(solution)/shard_map/dot_general | solution.py:58
  21.3 4.5 %all-to-all-start = ((s32[8,1,64]{2,1,0:T(1,128)}), s32[8,1,64]{2,1,0:T(1,128)S(1)}, u32[]{:S(2)}, u32[]{:S(2)}) async-start(s32[8,1,64]{2,1,0:T(1,128)} %all_to_all.9), calls=%async_computation | async-start | bytes 8192 | tf_op jit(solution)/shard_map/all_to_all | solution.py:69
  25.7 29.5 %all-reduce.2.cloned.1.call-done = bf16[256,1664]{1,0:T(8,128)(2,1)} async-done(((bf16[256,1664]{1,0:T(8,128)(2,1)}), bf16[256,1664]{1,0:T(8,128)(2,1)}) %all-reduce.2.cloned.1.call-update) | async-done | bytes 851984 | tf_op jit(solution)/shard_map/psum | solution.py:59
  55.3 3.6 convolution_convert_fusion.6
  59.0 5.5 %all-to-all-start.1 = ((bf16[8,64,1664]{2,1,0:T(8,128)(2,1)}), bf16[8,64,1664]{2,1,0:T(8,128)(2,1)S(1)}, u32[]{:S(2)}, u32[]{:S(2)}) async-start(bf16[8,64,1664]{2,1,0:T(8,128)(2,1)} %bitcast.4), calls=%async_computation.1 | async-start | bytes 3407872 | tf_op jit(solution)/shard_map/all_to_all | solution.py:73
  64.5 2.0 collective-permute-start.4
  66.6 1.9 collective-permute-start.6
  68.5 1.5 collective-permute-start.7
  72.7 31.8 %collective-permute-done.4 = bf16[208,2048]{1,0:T(8,128)(2,1)} collective-permute-done((bf16[208,2048]{1,0:T(8,128)(2,1)}, bf16[208,2048]{1,0:T(8,128)(2,1)}, u32[]{:S(2)}, u32[]{:S(2)}) %collective-permute-start.4) | collective-permute-done | bytes 852000 | tf_op jit(solution)/shard_map/ppermute | solution.py:34
  104.5 16.3 %collective-permute-done.5 = bf16[208,2048]{1,0:T(8,128)(2,1)} collective-permute-done((bf16[208,2048]{1,0:T(8,128)(2,1)}, bf16[208,2048]{1,0:T(8,128)(2,1)}, u32[]{:S(2)}, u32[]{:S(2)}) %collective-permute-start.5) | collective-permute-done | bytes 852000 | tf_op jit(solution)/shard_map/ppermute | solution.py:34
  120.8 11.0 %collective-permute-done.7 = bf16[208,2048]{1,0:T(8,128)(2,1)} collective-permute-done((bf16[208,2048]{1,0:T(8,128)(2,1)}, bf16[208,2048]{1,0:T(8,128)(2,1)}, u32[]{:S(2)}, u32[]{:S(2)}) %collective-permute-start.7) | collective-permute-done | bytes 852000 | tf_op jit(solution)/shard_map/ppermute | solution.py:38
  131.8 8.1 %all-to-all-done.1 = bf16[8,64,1664]{2,1,0:T(8,128)(2,1)S(1)} async-done(((bf16[8,64,1664]{2,1,0:T(8,128)(2,1)}), bf16[8,64,1664]{2,1,0:T(8,128)(2,1)S(1)}, u32[]{:S(2)}, u32[]{:S(2)}) %all-to-all-start.1) | async-done | bytes 1703968 | tf_op jit(solution)/shard_map/all_to_all | solution.py:73
  139.9 1.4 collective-permute-start.8
  142.9 4.4 %fusion.2 = (f32[1024]{0:T(1024)S(1)}, bf16[1024,1664]{1,0:T(8,128)(2,1)S(1)}) fusion(bf16[1024,1664]{1,0:T(8,128)(2,1)} %param.17, bf16[512,1664]{1,0:T(8,128)(2,1)S(1)} %bitcast.115, s32[512]{0:T(512)S(1)} %eq.58, pred[1024]{0:T(1024)(128)(4,1)S(1)} %fusion.100), kind=kOutput, calls=%fused_computation.10 | convolution fusion | flops 1753873408 | bytes 8526848 | tf_op jit(solution)/shard_map/dot_general | solution.py:79
  147.3 5.9 %convolution_convert_fusion = bf16[1024,1248]{0,1:T(8,128)(2,1)S(1)} fusion(bf16[1664,1248]{0,1:T(8,128)(2,1)S(1)} %copy-done.22, bf16[1024,1664]{1,0:T(8,128)(2,1)S(1)} %get-tuple-element.48, f32[1664]{0:T(1024)S(1)} %copy-done.23, f32[1024]{0:T(1024)S(1)} %add_rsqrt_fusion), kind=kOutput, calls=%fused_computation.61 | convolution fusion | flops 4261117952 | bytes 10127872 | tf_op jit(solution)/shard_map/dot_general | solution.py:84
  153.2 10.6 %collective-permute-done.10 = bf16[208,2048]{1,0:T(8,128)(2,1)S(1)} collective-permute-done((bf16[208,2048]{1,0:T(8,128)(2,1)}, bf16[208,2048]{1,0:T(8,128)(2,1)S(1)}, u32[]{:S(2)}, u32[]{:S(2)}) %collective-permute-start.10) | collective-permute-done | bytes 852000 | tf_op jit(solution)/shard_map/ppermute | solution.py:38
  163.8 14.7 %collective-permute-done.11 = bf16[208,2048]{1,0:T(8,128)(2,1)S(1)} collective-permute-done((bf16[208,2048]{1,0:T(8,128)(2,1)}, bf16[208,2048]{1,0:T(8,128)(2,1)S(1)}, u32[]{:S(2)}, u32[]{:S(2)}) %collective-permute-start.11) | collective-permute-done | bytes 852000 | tf_op jit(solution)/shard_map/ppermute | solution.py:38
  180.6 4.8 %slice_reduce_fusion.1 = (bf16[4,128,4,104]{1,0,3,2:T(4,128)(2,1)S(1)}, bf16[4,128,4,104]{1,0,3,2:T(4,128)(2,1)S(1)}) fusion(bf16[4,2,128,4,104]{2,1,0,4,3:T(2,128)(2,1)S(1)} %reshape_squeeze.10), kind=kLoop, calls=%fused_computation.148 | loop fusion | bytes 1703936 | tf_op jit(solution)/shard_map/slice | solution.py:94
  185.6 7.7 %fusion.185 = (f32[4,512]{1,0:T(4,128)S(1)}, f32[4,512,1024]{2,1,0:T(8,128)}) fusion(pred[512,1024]{1,0:T(8,128)(4,1)} %iota_compare_fusion, bf16[512,4,104]{0,2,1:T(8,128)(2,1)S(1)} %reshape_squeeze.12, bf16[1024,4,3,104]{0,3,2,1:T(8,128)(2,1)} %bitcast.119), kind=kOutput, calls=%fused_computation.267 | convolution fusion | flops 444597248 | bytes 10199040 | tf_op jit(solution)/shard_map/sub | solution.py:108
  193.3 5.2 %fusion.104 = bf16[4,104,512]{2,1,0:T(8,128)(2,1)S(1)} fusion(f32[4,512,1024]{2,1,0:T(8,128)} %get-tuple-element.52, f32[4,512]{1,0:T(4,128)S(1)} %get-tuple-element.51, bf16[1024,4,3,104]{0,3,2,1:T(8,128)(2,1)} %bitcast.120), kind=kOutput, calls=%fused_computation.141 | convolution fusion | flops 440614912 | bytes 9674752 | tf_op jit(solution)/shard_map/hqk,khd->qhd/dot_general | solution.py:110
  198.5 2.4 convolution_convert_fusion.2
  202.8 3.6 broadcast.214.clone
  206.5 1.5 bitcast_dynamic-update-slice_fusion
  208.2 7.6 %fusion.184 = (f32[4,512]{1,0:T(4,128)S(1)}, f32[4,512,1024]{2,1,0:T(8,128)}) fusion(pred[512,1024]{1,0:T(8,128)(4,1)S(1)} %iota_compare_fusion.1, bf16[512,4,104]{0,2,1:T(8,128)(2,1)S(1)} %reshape_squeeze.11, bf16[1024,4,3,104]{0,3,2,1:T(8,128)(2,1)} %bitcast.121), kind=kOutput, calls=%fused_computation.266 | convolution fusion | flops 444597248 | bytes 10199040 | tf_op jit(solution)/shard_map/sub | solution.py:108
  215.8 5.5 %fusion.105 = bf16[4,104,512]{2,1,0:T(8,128)(2,1)S(1)} fusion(f32[4,512,1024]{2,1,0:T(8,128)} %get-tuple-element.50, f32[4,512]{1,0:T(4,128)S(1)} %get-tuple-element.49, bf16[1024,4,3,104]{0,3,2,1:T(8,128)(2,1)} %bitcast.122), kind=kOutput, calls=%fused_computation.142 | convolution fusion | flops 440614912 | bytes 9674752 | tf_op jit(solution)/shard_map/hqk,khd->qhd/dot_general | solution.py:110
  221.3 2.4 convolution_convert_fusion.3
  223.7 2.9 bitcast_dynamic-update-slice_fusion.7
  228.6 2.2 bitcast_dynamic-update-slice_fusion.12
  230.7 2.1 bitcast_dynamic-update-slice_fusion.11
  232.9 2.2 bitcast_dynamic-update-slice_fusion.5
  235.1 2.2 bitcast_dynamic-update-slice_fusion.4
  237.3 3.3 collective-permute-start.12
  240.6 21.1 %reduce-scatter.5.cloned.1.call-done = bf16[128,1664]{1,0:T(8,128)(2,1)} async-done(((bf16[512,1664]{1,0:T(8,128)(2,1)}), bf16[128,1664]{1,0:T(8,128)(2,1)}) %reduce-scatter.5.cloned.1.call-update) | async-done | bytes 426000 | tf_op jit(solution)/shard_map/reduce_scatter | solution.py:116
  261.7 1.7 multiply_reduce_fusion.1
  263.5 2.6 multiply_convert_fusion.1
  268.2 2.2 bitcast_dynamic-update-slice_fusion.3
  271.3 2.2 bitcast_dynamic-update-slice_fusion.8
  273.5 2.4 collective-permute-done.13
  275.9 2.2 bitcast_dynamic-update-slice_fusion.1
  278.4 8.3 %all-gather.5.cloned.1.call-done = bf16[512,1664]{1,0:T(8,128)(2,1)} async-done(((bf16[128,1664]{1,0:T(8,128)(2,1)}), bf16[512,1664]{1,0:T(8,128)(2,1)}) %all-gather.5.cloned.1.call-update) | async-done | bytes 1703952 | tf_op jit(solution)/shard_map/all_gather | solution.py:128
  286.7 21.2 %convolution_convert_fusion.4 = bf16[512,1664]{1,0:T(8,128)(2,1)} fusion(bf16[1664,2048]{1,0:T(8,128)(2,1)} %bitcast.29, bf16[512,1664]{1,0:T(8,128)(2,1)} %all-gather.5.cloned.1.call-done, bf16[1664,2048]{1,0:T(8,128)(2,1)} %bitcast.113), kind=kOutput, calls=%fused_computation.68 | convolution fusion | flops 7048331264 | bytes 17039360 | tf_op jit(solution)/shard_map/dot_general | solution.py:135
  308.6 21.1 %convolution_convert_fusion.5 = bf16[512,1664]{1,0:T(8,128)(2,1)} fusion(bf16[1664,2048]{1,0:T(8,128)(2,1)} %bitcast.29, bf16[512,1664]{1,0:T(8,128)(2,1)} %all-gather.3.cloned.1.call-done, bf16[1664,2048]{1,0:T(8,128)(2,1)} %bitcast.114), kind=kOutput, calls=%fused_computation.69 | convolution fusion | flops 7048331264 | bytes 17039360 | tf_op jit(solution)/shard_map/dot_general | solution.py:135
  330.4 9.7 %reduce-scatter.11.cloned.1.call-done = bf16[128,1664]{1,0:T(8,128)(2,1)} async-done(((bf16[512,1664]{1,0:T(8,128)(2,1)}), bf16[128,1664]{1,0:T(8,128)(2,1)}) %reduce-scatter.11.cloned.1.call-update) | async-done | bytes 426000 | tf_op jit(solution)/shard_map/reduce_scatter | solution.py:138
  340.2 31.6 %reduce-scatter.7.cloned.1.call-done = bf16[128,1664]{1,0:T(8,128)(2,1)} async-done(((bf16[512,1664]{1,0:T(8,128)(2,1)}), bf16[128,1664]{1,0:T(8,128)(2,1)}) %reduce-scatter.7.cloned.1.call-update) | async-done | bytes 426000 | tf_op jit(solution)/shard_map/reduce_scatter | solution.py:138
  371.7 1.9 select_convert_fusion.1
  (110 shorter events, 18.7 us)
Async XLA Ops:
  6.5 192.0 %copy-start = (bf16[416,1664]{1,0:T(8,128)(2,1)S(1)}, bf16[416,1664]{1,0:T(8,128)(2,1)}, u32[]{:S(2)}) copy-start(bf16[416,1664]{1,0:T(8,128)(2,1)} %param.20) | copy-start | bytes 4153348
  6.5 48.7 %all-reduce.2.cloned.1.call-start = ((), (), s32[]{:S(2)}) async-start(), calls=%async_computation.6 | async-start | bytes 1703936 | tf_op jit(solution)/shard_map/psum | solution.py:59
  6.5 48.7 %collective-permute-start.1 = (bf16[208,2048]{1,0:T(8,128)(2,1)}, bf16[208,2048]{1,0:T(8,128)(2,1)}, u32[]{:S(2)}, u32[]{:S(2)}) collective-permute-start(bf16[208,2048]{1,0:T(8,128)(2,1)} %bitcast.116), channel_id=1, source_target_pairs={{0,4},{4,0},{8,12},{12,8},{16,20},{20,16},{24,28},{28,24},{1,5},{5... | collective-permute-start | bytes 2555912 | tf_op jit(solution)/shard_map/ppermute | solution.py:34
  9.5 45.8 %collective-permute-start.3 = (bf16[208,2048]{1,0:T(8,128)(2,1)}, bf16[208,2048]{1,0:T(8,128)(2,1)S(1)}, u32[]{:S(2)}, u32[]{:S(2)}) collective-permute-start(bf16[208,2048]{1,0:T(8,128)(2,1)} %bitcast.117), channel_id=1, source_target_pairs={{0,8},{4,12},{8,16},{12,20},{16,24},{20,28},{24,0},{28,4},{1,9},{5... | collective-permute-start | bytes 2555912 | tf_op jit(solution)/shard_map/ppermute | solution.py:38
  11.1 44.2 %collective-permute-start = (bf16[208,2048]{1,0:T(8,128)(2,1)}, bf16[208,2048]{1,0:T(8,128)(2,1)}, u32[]{:S(2)}, u32[]{:S(2)}) collective-permute-start(bf16[208,2048]{1,0:T(8,128)(2,1)} %param.22), channel_id=1, source_target_pairs={{0,4},{4,0},{8,12},{12,8},{16,20},{20,16},{24,28},{28,24},{1,5},{5... | collective-permute-start | bytes 2555912 | tf_op jit(solution)/shard_map/ppermute | solution.py:34
  11.6 43.7 %collective-permute-start.2 = (bf16[208,2048]{1,0:T(8,128)(2,1)}, bf16[208,2048]{1,0:T(8,128)(2,1)S(1)}, u32[]{:S(2)}, u32[]{:S(2)}) collective-permute-start(bf16[208,2048]{1,0:T(8,128)(2,1)} %param.22), channel_id=1, source_target_pairs={{0,8},{4,12},{8,16},{12,20},{16,24},{20,28},{24,0},{28,4},{1,9},{5... | collective-permute-start | bytes 2555912 | tf_op jit(solution)/shard_map/ppermute | solution.py:38
  14.6 5.7 %copy-start.21 = (s32[256]{0:T(256)S(1)}, s32[256]{0:T(256)}, u32[]{:S(2)}) copy-start(s32[256]{0:T(256)} %param.15) | copy-start | bytes 3076
  21.3 37.7 %all-to-all-start = ((s32[8,1,64]{2,1,0:T(1,128)}), s32[8,1,64]{2,1,0:T(1,128)S(1)}, u32[]{:S(2)}, u32[]{:S(2)}) async-start(s32[8,1,64]{2,1,0:T(1,128)} %all_to_all.9), calls=%async_computation | async-start | bytes 8192 | tf_op jit(solution)/shard_map/all_to_all | solution.py:69
  55.3 3.7 copy-start.8
  55.3 3.6 copy-start.10
  59.0 80.9 %all-to-all-start.1 = ((bf16[8,64,1664]{2,1,0:T(8,128)(2,1)}), bf16[8,64,1664]{2,1,0:T(8,128)(2,1)S(1)}, u32[]{:S(2)}, u32[]{:S(2)}) async-start(bf16[8,64,1664]{2,1,0:T(8,128)(2,1)} %bitcast.4), calls=%async_computation.1 | async-start | bytes 3407872 | tf_op jit(solution)/shard_map/all_to_all | solution.py:73
  64.5 176.2 %reduce-scatter.9.cloned.1.call-start = ((), (), s32[]{:S(2)}) async-start(), calls=%async_computation.10 | async-start | bytes 2129920 | tf_op jit(solution)/shard_map/reduce_scatter | solution.py:116
  64.5 40.0 %collective-permute-start.4 = (bf16[208,2048]{1,0:T(8,128)(2,1)}, bf16[208,2048]{1,0:T(8,128)(2,1)}, u32[]{:S(2)}, u32[]{:S(2)}) collective-permute-start(bf16[208,2048]{1,0:T(8,128)(2,1)} %copy-done.10), channel_id=1, source_target_pairs={{0,4},{4,0},{8,12},{12,8},{16,20},{20,16},{24,28},{28,24},{1,5},{5... | collective-permute-start | bytes 2555912 | tf_op jit(solution)/shard_map/ppermute | solution.py:34
  66.5 54.3 %collective-permute-start.5 = (bf16[208,2048]{1,0:T(8,128)(2,1)}, bf16[208,2048]{1,0:T(8,128)(2,1)}, u32[]{:S(2)}, u32[]{:S(2)}) collective-permute-start(bf16[208,2048]{1,0:T(8,128)(2,1)} %copy-done.8), channel_id=1, source_target_pairs={{0,4},{4,0},{8,12},{12,8},{16,20},{20,16},{24,28},{28,24},{1,5},{5... | collective-permute-start | bytes 2555912 | tf_op jit(solution)/shard_map/ppermute | solution.py:34
  66.6 54.2 %collective-permute-start.6 = (bf16[208,2048]{1,0:T(8,128)(2,1)}, bf16[208,2048]{1,0:T(8,128)(2,1)}, u32[]{:S(2)}, u32[]{:S(2)}) collective-permute-start(bf16[208,2048]{1,0:T(8,128)(2,1)} %copy-done.10), channel_id=1, source_target_pairs={{0,8},{4,12},{8,16},{12,20},{16,24},{20,28},{24,0},{28,4},{1,9},{5... | collective-permute-start | bytes 2555912 | tf_op jit(solution)/shard_map/ppermute | solution.py:38
  68.5 63.3 %collective-permute-start.7 = (bf16[208,2048]{1,0:T(8,128)(2,1)}, bf16[208,2048]{1,0:T(8,128)(2,1)}, u32[]{:S(2)}, u32[]{:S(2)}) collective-permute-start(bf16[208,2048]{1,0:T(8,128)(2,1)} %copy-done.8), channel_id=1, source_target_pairs={{0,8},{4,12},{8,16},{12,20},{16,24},{20,28},{24,0},{28,4},{1,9},{5... | collective-permute-start | bytes 2555912 | tf_op jit(solution)/shard_map/ppermute | solution.py:38
  139.9 23.9 %collective-permute-start.10 = (bf16[208,2048]{1,0:T(8,128)(2,1)}, bf16[208,2048]{1,0:T(8,128)(2,1)S(1)}, u32[]{:S(2)}, u32[]{:S(2)}) collective-permute-start(bf16[208,2048]{1,0:T(8,128)(2,1)} %collective-permute-done.6), channel_id=1, source_target_pairs={{0,8},{4,12},{8,16},{12,20},{16,24},{20,28},{24,0},{28,4},{1,9},{5... | collective-permute-start | bytes 2555912 | tf_op jit(solution)/shard_map/ppermute | solution.py:38
  139.9 38.6 %collective-permute-start.8 = (bf16[208,2048]{1,0:T(8,128)(2,1)}, bf16[208,2048]{1,0:T(8,128)(2,1)S(1)}, u32[]{:S(2)}, u32[]{:S(2)}) collective-permute-start(bf16[208,2048]{1,0:T(8,128)(2,1)} %collective-permute-done.6), channel_id=1, source_target_pairs={{0,4},{4,0},{8,12},{12,8},{16,20},{20,16},{24,28},{28,24},{1,5},{5... | collective-permute-start | bytes 2555912 | tf_op jit(solution)/shard_map/ppermute | solution.py:34
  141.3 37.2 %collective-permute-start.11 = (bf16[208,2048]{1,0:T(8,128)(2,1)}, bf16[208,2048]{1,0:T(8,128)(2,1)S(1)}, u32[]{:S(2)}, u32[]{:S(2)}) collective-permute-start(bf16[208,2048]{1,0:T(8,128)(2,1)} %collective-permute-done.7), channel_id=1, source_target_pairs={{0,8},{4,12},{8,16},{12,20},{16,24},{20,28},{24,0},{28,4},{1,9},{5... | collective-permute-start | bytes 2555912 | tf_op jit(solution)/shard_map/ppermute | solution.py:38
  142.6 35.9 %collective-permute-start.9 = (bf16[208,2048]{1,0:T(8,128)(2,1)}, bf16[208,2048]{1,0:T(8,128)(2,1)S(1)}, u32[]{:S(2)}, u32[]{:S(2)}) collective-permute-start(bf16[208,2048]{1,0:T(8,128)(2,1)} %collective-permute-done.7), channel_id=1, source_target_pairs={{0,4},{4,0},{8,12},{12,8},{16,20},{20,16},{24,28},{28,24},{1,5},{5... | collective-permute-start | bytes 2555912 | tf_op jit(solution)/shard_map/ppermute | solution.py:34
  142.9 4.5 %copy-start.22 = (bf16[1664,1248]{0,1:T(8,128)(2,1)S(1)}, bf16[1664,1248]{0,1:T(8,128)(2,1)}, u32[]{:S(2)}) copy-start(bf16[1664,1248]{0,1:T(8,128)(2,1)} %param.19) | copy-start | bytes 12460036
  142.9 4.5 %copy-start.23 = (f32[1664]{0:T(1024)S(1)}, f32[1664]{0:T(1024)}, u32[]{:S(2)}) copy-start(f32[1664]{0:T(1024)} %param.18) | copy-start | bytes 19972
  147.3 5.9 %copy-start.5 = (bf16[1024,1664]{1,0:T(8,128)(2,1)}, bf16[1024,1664]{1,0:T(8,128)(2,1)S(1)}, u32[]{:S(2)}) copy-start(bf16[1024,1664]{1,0:T(8,128)(2,1)S(1)} %get-tuple-element.48) | copy-start | bytes 10223620
  153.2 25.3 %copy-start.19 = (bf16[1024,1248]{0,1:T(8,128)(2,1)}, bf16[1024,1248]{0,1:T(8,128)(2,1)S(1)}, u32[]{:S(2)}) copy-start(bf16[1024,1248]{0,1:T(8,128)(2,1)S(1)} %convolution_convert_fusion) | copy-start | bytes 7667716
  163.8 14.7 %copy-start.12 = (bf16[208,2048]{1,0:T(8,128)(2,1)}, bf16[208,2048]{1,0:T(8,128)(2,1)S(1)}, u32[]{:S(2)}) copy-start(bf16[208,2048]{1,0:T(8,128)(2,1)S(1)} %collective-permute-done.10) | copy-start | bytes 2555908
  178.5 0.9 copy-start.14
  178.5 1.2 copy-start.16
  178.5 1.5 copy-start.18
  200.9 1.8 copy-start.6
  200.9 60.8 %reduce-scatter.5.cloned.1.call-start = ((), (), s32[]{:S(2)}) async-start(), calls=%async_computation.7 | async-start | bytes 2129920 | tf_op jit(solution)/shard_map/reduce_scatter | solution.py:116
  202.7 3.8 copy-start.7
  202.8 5.2 %copy-start.2 = (bf16[8,208,2048]{2,1,0:T(8,128)(2,1)}, bf16[8,208,2048]{2,1,0:T(8,128)(2,1)S(1)}, u32[]{:S(2)}) copy-start(bf16[8,208,2048]{2,1,0:T(8,128)(2,1)S(1)} %bitcast_dynamic-update-slice_fusion.15) | copy-start | bytes 20447236
  223.7 3.0 copy-start.11
  223.7 4.0 %copy-start.9 = (bf16[208,2048]{1,0:T(8,128)(2,1)S(1)}, bf16[208,2048]{1,0:T(8,128)(2,1)}, u32[]{:S(2)}) copy-start(bf16[208,2048]{1,0:T(8,128)(2,1)} %copy-done.8) | copy-start | bytes 2555908
  223.7 63.0 %all-gather.5.cloned.1.call-start = ((), (), s32[]{:S(2)}) async-start(), calls=%async_computation.11 | async-start | bytes 2129920 | tf_op jit(solution)/shard_map/all_gather | solution.py:128
  227.6 9.7 %copy-start.13 = (bf16[208,2048]{1,0:T(8,128)(2,1)S(1)}, bf16[208,2048]{1,0:T(8,128)(2,1)}, u32[]{:S(2)}) copy-start(bf16[208,2048]{1,0:T(8,128)(2,1)} %copy-done.12) | copy-start | bytes 2555908
  227.6 12.9 %copy-start.15 = (bf16[208,2048]{1,0:T(8,128)(2,1)S(1)}, bf16[208,2048]{1,0:T(8,128)(2,1)}, u32[]{:S(2)}) copy-start(bf16[208,2048]{1,0:T(8,128)(2,1)} %copy-done.14) | copy-start | bytes 2555908
  228.6 34.9 %copy-start.20 = (f32[1664]{0:T(1024)S(1)}, f32[1664]{0:T(1024)}, u32[]{:S(2)}) copy-start(f32[1664]{0:T(1024)} %param.21) | copy-start | bytes 19972
  232.9 33.3 %copy-start.17 = (bf16[208,2048]{1,0:T(8,128)(2,1)S(1)}, bf16[208,2048]{1,0:T(8,128)(2,1)}, u32[]{:S(2)}) copy-start(bf16[208,2048]{1,0:T(8,128)(2,1)} %copy-done.16) | copy-start | bytes 2555908
  237.3 34.0 %collective-permute-start.12 = (bf16[208,2048]{1,0:T(8,128)(2,1)S(1)}, bf16[208,2048]{1,0:T(8,128)(2,1)}, u32[]{:S(2)}, u32[]{:S(2)}) collective-permute-start(bf16[208,2048]{1,0:T(8,128)(2,1)S(1)} %copy-done.13), channel_id=1, source_target_pairs={{0,4},{4,0},{8,12},{12,8},{16,20},{20,16},{24,28},{28,24},{1,5},{5... | collective-permute-start | bytes 2555912 | tf_op jit(solution)/shard_map/ppermute | solution.py:34
  240.6 35.4 %collective-permute-start.13 = (bf16[208,2048]{1,0:T(8,128)(2,1)S(1)}, bf16[208,2048]{1,0:T(8,128)(2,1)}, u32[]{:S(2)}, u32[]{:S(2)}) collective-permute-start(bf16[208,2048]{1,0:T(8,128)(2,1)S(1)} %copy-done.15), channel_id=1, source_target_pairs={{0,4},{4,0},{8,12},{12,8},{16,20},{20,16},{24,28},{28,24},{1,5},{5... | collective-permute-start | bytes 2555912 | tf_op jit(solution)/shard_map/ppermute | solution.py:34
  266.1 42.5 %all-gather.3.cloned.1.call-start = ((), (), s32[]{:S(2)}) async-start(), calls=%async_computation.8 | async-start | bytes 2129920 | tf_op jit(solution)/shard_map/all_gather | solution.py:128
  278.1 62.0 %reduce-scatter.11.cloned.1.call-start = ((), (), s32[]{:S(2)}) async-start(), calls=%async_computation.12 | async-start | bytes 2129920 | tf_op jit(solution)/shard_map/reduce_scatter | solution.py:138
  307.9 63.8 %copy-start.3 = (bf16[128,1664]{1,0:T(8,128)(2,1)S(1)}, bf16[128,1664]{1,0:T(8,128)(2,1)}, u32[]{:S(2)}) copy-start(bf16[128,1664]{1,0:T(8,128)(2,1)} %reduce-scatter.9.cloned.1.call-done) | copy-start | bytes 1277956
  307.9 63.8 %copy-start.4 = (bf16[128,1664]{1,0:T(8,128)(2,1)S(1)}, bf16[128,1664]{1,0:T(8,128)(2,1)}, u32[]{:S(2)}) copy-start(bf16[128,1664]{1,0:T(8,128)(2,1)} %reduce-scatter.5.cloned.1.call-done) | copy-start | bytes 1277956
  307.9 63.8 %reduce-scatter.7.cloned.1.call-start = ((), (), s32[]{:S(2)}) async-start(), calls=%async_computation.9 | async-start | bytes 2129920 | tf_op jit(solution)/shard_map/reduce_scatter | solution.py:138
  308.6 66.0 %copy-start.1 = (bf16[416,1664]{1,0:T(8,128)(2,1)S(1)}, bf16[416,1664]{1,0:T(8,128)(2,1)}, u32[]{:S(2)}) copy-start(bf16[416,1664]{1,0:T(8,128)(2,1)} %param.20) | copy-start | bytes 4153348
Sparse Core Ops, SparseCore 0:
  20.4 34.8 all-reduce.1
  201.0 29.0 reduce-scatter.8
  232.7 28.9 reduce-scatter.4
  266.2 20.3 all-gather.4
  288.1 20.3 all-gather.2
  311.2 28.9 reduce-scatter.10
  342.7 28.9 reduce-scatter.6
